TPU v7x, 256 devices: a whole 4x4x8 slice. The times are simulated.
256 devices in a mesh: tm: 8 (over x_hi, y), row: 32 (over x_lo, z, core).
Axes of the slice: x: 4 (x_hi: 2, x_lo: 2; x = x_hi * 2 + x_lo), y: 4, z: 8, core: 2. Of those that a mesh axis runs over, the one named last changes fastest.
Arguments:
- voltage: bfloat16 [128, 128, 128, 512], P('tm', 'row'), may hold values from -6 to 6
Outputs:
- beam_power: float32 [8, 256, 128, 128], P('tm', 'row')
All inputs are finite; a program needn't handle non-finite values.
Results may differ from a plain program's by a relative error of at most 0.0041.
Values may be sent and summed in bfloat16 or wider, within the bound.
A program may use at most 128 MiB of HBM per device.

v0:
```python
import math

import jax
import jax.numpy as jnp
from jax import lax
from jax.sharding import PartitionSpec as P

R = 128
TAPS = 4


def shifted(value, axis, steps):
    count = lax.axis_size(axis)
    pairs = [(source, (source + steps) % count) for source in range(count)]
    return lax.ppermute(value, axis, pairs)


def pfb_window(taps, channels):
    points = jnp.arange(taps * channels, dtype=jnp.float32)
    offset = (points + 0.5) / channels - taps / 2.0
    taper = 0.5 - 0.5 * jnp.cos(2.0 * math.pi * (points + 0.5) / (taps * channels))
    shaped = (jnp.sinc(offset) * taper).reshape(taps, channels)
    return jnp.concatenate([shaped, shaped], axis=1)


def dft_table(length):
    indices = jnp.arange(length, dtype=jnp.int32)
    products = indices[:, None] * indices[None, :] % length
    phase_angle = products.astype(jnp.float32) * (2.0 * math.pi / length)
    norm_scale = 1.0 / math.sqrt(length)
    cosine = jnp.cos(phase_angle) * norm_scale
    sine = jnp.sin(phase_angle) * norm_scale
    upper = jnp.stack([cosine, -sine], axis=1)
    bottom = jnp.stack([sine, cosine], axis=1)
    return jnp.stack([upper, bottom], axis=0).astype(jnp.bfloat16)


def body(voltage):
    count_frames, rows_here, columns, width = voltage.shape
    channels = width // 2
    history = TAPS - 1
    weights = pfb_window(TAPS, channels)
    earlier = shifted(voltage[count_frames - history :], "tm", 1)
    extended = jnp.concatenate([earlier, voltage], axis=0)
    summed = weights[0] * extended[0:count_frames].astype(jnp.float32)
    for tap_index in range(1, TAPS):
        summed = summed + weights[tap_index] * extended[
            tap_index : tap_index + count_frames
        ].astype(jnp.float32)
    weighted = summed.astype(jnp.bfloat16)
    fine_table = dft_table(channels).reshape(width, width)
    spectrum = jnp.einsum("fdcs,sq->fdqc", weighted, fine_table, preferred_element_type=jnp.float32)
    spectrum = spectrum.astype(jnp.bfloat16).reshape(count_frames, rows_here, 2, channels, columns)
    column_table = dft_table(columns)
    row_table = dft_table(R)
    column_beam = jnp.einsum(
        "frpkc,pcqv->frqkv",
        lax.all_to_all(spectrum, "row", split_axis=3, concat_axis=1, tiled=True),
        column_table,
        preferred_element_type=jnp.float32,
    )
    row_column_beam = column_beam.astype(jnp.bfloat16)
    beam_field = jnp.einsum(
        "frqkv,qrsu->fskuv", row_column_beam, row_table, preferred_element_type=jnp.float32
    )
    per_frame = jnp.sum(beam_field * beam_field, axis=1)
    power_sum = jnp.sum(per_frame, axis=0) / count_frames
    return power_sum[None]


def solution(mesh):
    return jax.shard_map(
        body,
        mesh=mesh,
        in_specs=(P("tm", "row", None, None),),
        out_specs=P("tm", "row", None, None),
        check_vma=False,
    )
```

profile of v0, /device:TPU:1, one launch (start us, length us, event | category | flops | bytes accessed | tf_op | source)
XLA Modules:
  0.0 312.7 jit_solution(17736124760358965129)
XLA Ops:
  0.0 2.7 slice.25
  2.7 2.1 collective-permute-start
  4.8 1.0 fusion.26
  5.8 1.1 negate_convert_fusion
  6.9 0.1 pad_maximum_fusion
  7.0 0.5 copy.12
  7.5 0.3 reshape.184
  7.8 0.1 fusion.42
  7.9 33.1 %collective-permute-done = bf16[3,4,128,512]{3,2,1,0:T(8,128)(2,1)S(1)} collective-permute-done((bf16[3,4,128,512]{3,2,1,0:T(8,128)(2,1)}, bf16[3,4,128,512]{3,2,1,0:T(8,128)(2,1)S(1)}, u32[]{:S(2)}, u32[]{:S(2)}) %collective-permute-start) | collective-permute-done | bytes 1572896 | tf_op jit(solution)/shard_map/ppermute | solution.py:15
  41.0 1.3 constant_dynamic-update-slice_fusion.1
  42.4 7.7 %constant_dynamic-update-slice_fusion = bf16[19,4,128,512]{3,2,1,0:T(8,128)(2,1)} fusion(bf16[19,4,128,512]{3,2,1,0:T(8,128)(2,1)} %constant_dynamic-update-slice_fusion.1, bf16[16,4,128,512]{3,2,1,0:T(8,128)(2,1)} %param.1), kind=kLoop, calls=%fused_computation.59 | loop fusion | bytes 16777216 | tf_op jit(solution)/shard_map/concatenate | solution.py:44
  50.1 16.7 %fusion.12 = bf16[512,16,4,128]{3,0,2,1:T(8,128)(2,1)} fusion(bf16[16,4,128,512]{3,2,1,0:T(8,128)(2,1)} %param.1, bf16[19,4,128,512]{3,2,1,0:T(8,128)(2,1)} %constant_dynamic-update-slice_fusion, f32[512]{0:T(512)S(1)} %bitcast.67, f32[512]{0:T(512)S(1)} %bitcast.69, f32[512]{0:T(512)S(1)} %bitcast.68, f32[512]{0:T(512)S(1)} %bitcast.66, ...), kind=kOutput, calls=%fused_computation.16 | convolution fusion | flops 4349493248 | bytes 42475520 | tf_op jit(solution)/shard_map/fdcs,sq->fdqc/dot_general | solution.py:52
  66.8 13.1 %copy.13 = bf16[16,4,2,256,128]{4,2,1,0,3:T(2,128)(2,1)} copy(bf16[16,4,2,256,128]{4,3,2,1,0:T(8,128)(2,1)} %bitcast.64) | data formatting | bytes 16777216 | tf_op jit(solution)/shard_map/reshape | solution.py:53
  80.0 12.9 %all-to-all-start = ((bf16[16,4,2,256,128]{4,2,1,0,3:T(2,128)(2,1)}), bf16[16,4,2,256,128]{4,2,1,0,3:T(2,128)(2,1)}, u32[]{:S(2)}, u32[]{:S(2)}) async-start(bf16[16,4,2,256,128]{4,2,1,0,3:T(2,128)(2,1)} %copy.13), calls=%async_computation | async-start | bytes 16777216 | tf_op jit(solution)/shard_map/all_to_all | solution.py:58
  92.9 0.3 fusion.36
  93.1 0.3 negate_convert_fusion.1
  93.5 183.3 %all-to-all-done = bf16[16,4,2,256,128]{4,2,1,0,3:T(2,128)(2,1)} async-done(((bf16[16,4,2,256,128]{4,2,1,0,3:T(2,128)(2,1)}), bf16[16,4,2,256,128]{4,2,1,0,3:T(2,128)(2,1)}, u32[]{:S(2)}, u32[]{:S(2)}) %all-to-all-start) | async-done | bytes 8388640 | tf_op jit(solution)/shard_map/all_to_all | solution.py:58
  276.8 16.3 %copy.35 = bf16[16,4,2,256,128]{4,3,2,1,0:T(8,128)(2,1)} copy(bf16[16,4,2,256,128]{4,2,1,0,3:T(2,128)(2,1)} %all-to-all-done) | data formatting | bytes 16777216 | tf_op jit(solution)/shard_map/all_to_all | solution.py:58
  293.1 9.2 %copy.15 = bf16[16,32,4,2,8,128]{5,4,3,2,1,0:T(8,128)(2,1)} copy(bf16[16,32,4,2,8,128]{5,4,1,3,2,0:T(8,128)(2,1)} %bitcast.63) | data formatting | bytes 16777216 | tf_op jit(solution)/shard_map/all_to_all | solution.py:58
  302.3 9.5 %fusion = f32[128,8,128]{2,0,1:T(8,128)S(1)} fusion(bf16[16,128,2,8,128,1]{4,3,2,1,0,5:T(8,128)(2,1)} %bitcast.65, bf16[1,128,2,128]{1,3,0,2:T(8,128)(2,1)S(1)} %get-tuple-element.8, bf16[1,128,2,128]{1,3,0,2:T(8,128)(2,1)S(1)} %get-tuple-element.7), kind=kOutput, calls=%fused_computation.1 | convolution fusion | flops 4307943424 | bytes 9043968 | tf_op jit(solution)/shard_map/frqkv,qrsu->fskuv/dot_general | solution.py:63
  311.8 0.8 multiply_bitcast_fusion
  (3 shorter events, 0.1 us)
Async XLA Ops:
  2.7 38.4 %collective-permute-start = (bf16[3,4,128,512]{3,2,1,0:T(8,128)(2,1)}, bf16[3,4,128,512]{3,2,1,0:T(8,128)(2,1)S(1)}, u32[]{:S(2)}, u32[]{:S(2)}) collective-permute-start(bf16[3,4,128,512]{3,2,1,0:T(8,128)(2,1)} %slice.25), channel_id=1, source_target_pairs={{0,32},{32,64},{64,96},{96,128},{128,160},{160,192},{192,224},{224... | collective-permute-start | bytes 4718600 | tf_op jit(solution)/shard_map/ppermute | solution.py:15
  80.0 196.8 %all-to-all-start = ((bf16[16,4,2,256,128]{4,2,1,0,3:T(2,128)(2,1)}), bf16[16,4,2,256,128]{4,2,1,0,3:T(2,128)(2,1)}, u32[]{:S(2)}, u32[]{:S(2)}) async-start(bf16[16,4,2,256,128]{4,2,1,0,3:T(2,128)(2,1)} %copy.13), calls=%async_computation | async-start | bytes 16777216 | tf_op jit(solution)/shard_map/all_to_all | solution.py:58
where the time goes:
time: 315 us; the launch traced here: 313 us
  waiting for transfers between devices  216 us (69%)
  local copies, waits for them, and re-layouts  51.2 us (16%)
  matrix products  26.3 us (8%)
  starting transfers between devices  15 us (5%)
  other arithmetic  3.66 us (1%)
    all_to_all x1, waiting for transfers between devices, body(): lax.all_to_all(spectrum, 'row', split_axis=3, concat_axis=1, tiled=True)  183 us
    ppermute x1, waiting for transfers between devices, shifted(): return lax.ppermute(value, axis, pairs)  33.1 us
    all_to_all x2, local copies, waits for them, and re-layouts, body(): lax.all_to_all(spectrum, 'row', split_axis=3, concat_axis=1, tiled=True)  25.5 us
    dot_general x1, matrix products, body(): jnp.einsum('fdcs,sq->fdqc', weighted, fine_table, preferred_element_type=...  16.7 us
    reshape x1, local copies, waits for them, and re-layouts, body(): spectrum.astype(jnp.bfloat16)  13.1 us
    all_to_all x1, starting transfers between devices, body(): lax.all_to_all(spectrum, 'row', split_axis=3, concat_axis=1, tiled=True)  12.9 us
    dot_general x1, matrix products, body(): jnp.einsum('frqkv,qrsu->fskuv', row_column_beam, row_table, preferred_ele...  9.54 us
    concatenate x1, local copies, waits for them, and re-layouts, body(): extended = jnp.concatenate([earlier, voltage], axis=0)  7.72 us
  transfers between devices with their start and end apart: 2, of which 2 were waited for; matrix products, arithmetic and copies ran while one was open for 1% of the time, Pallas kernels for 0%

commit v1 on v0

v1 whole, which is shorter than its diff:
```python
import math

import jax
import jax.numpy as jnp
import ml_dtypes
import numpy as np
from jax import lax
from jax.experimental import pallas as pl
from jax.experimental.pallas import tpu as pltpu
from jax.sharding import PartitionSpec as P

TAPS = 4
HISTORY = TAPS - 1
NCH = 256
C = 128
R = 128
FR = 16
NROW = 32
NTM = 8
RHERE = R // NROW
KHERE = NCH // NROW
RK = RHERE * KHERE
MESH_ID = pl.DeviceIdType.MESH


def pfb_window():
    points = np.arange(TAPS * NCH, dtype=np.float64)
    offset = (points + 0.5) / NCH - TAPS / 2.0
    taper = 0.5 - 0.5 * np.cos(2.0 * math.pi * (points + 0.5) / (TAPS * NCH))
    shaped = (np.sinc(offset) * taper).reshape(TAPS, NCH)
    return np.concatenate([shaped, shaped], axis=1).astype(np.float32)


def dft_table(length):
    indices = np.arange(length)
    angle = (indices[:, None] * indices[None, :] % length) * (2.0 * math.pi / length)
    cosine = np.cos(angle) / math.sqrt(length)
    sine = np.sin(angle) / math.sqrt(length)
    upper = np.stack([cosine, -sine], axis=1)
    bottom = np.stack([sine, cosine], axis=1)
    return np.stack([upper, bottom], axis=0).astype(np.float32).astype(ml_dtypes.bfloat16)


def tables():
    fine = dft_table(NCH).reshape(2 * NCH, 2, NROW, KHERE).transpose(2, 1, 3, 0)
    fine = fine.reshape(2 * NCH, 2 * NCH)
    column = dft_table(C).reshape(2 * C, 2 * C)
    row = dft_table(R).transpose(2, 3, 0, 1).reshape(2 * R, 2 * R)
    return fine, column, row


def kernel(
    volt_hbm, w_hbm, fine_hbm, col_hbm, row_hbm, out_hbm,
    volt, w, fine, col, row, weighted, send, recv, mid, acc,
    load_sem, table_sem, halo_sem, send_sem, recv_sem, out_sem,
):
    tm = lax.axis_index("tm")
    me = lax.axis_index("row")
    x, z, core = me // 16, (me // 2) % 8, me % 2
    after, before = (tm + 1) % NTM, (tm + NTM - 1) % NTM

    def partner(e):
        dz = (3 * (e // 4 + 1)) % 8
        dx = 1 - (e // 2) % 2
        dc = 1 - e % 2
        return (((x + dx) % 2) * 8 + (z + dz) % 8) * 2 + (core + dc) % 2

    barrier = pltpu.get_barrier_semaphore()

    def greet(e, carry):
        pl.semaphore_signal(barrier, inc=1, device_id={"row": partner(e)}, device_id_type=MESH_ID)
        return carry

    lax.fori_loop(0, NROW - 1, greet, 0)
    for neighbour in (before, after):
        pl.semaphore_signal(barrier, inc=1, device_id={"tm": neighbour}, device_id_type=MESH_ID)

    def load(g):
        return pltpu.make_async_copy(volt_hbm.at[g], volt.at[g + HISTORY], load_sem.at[g])

    table_copies = [
        pltpu.make_async_copy(a, b, table_sem.at[i])
        for i, (a, b) in enumerate(
            ((w_hbm, w), (fine_hbm, fine), (col_hbm, col), (row_hbm, row))
        )
    ]
    table_copies[0].start()
    for g in range(TAPS):
        load(g).start()
    for copy in table_copies[1:]:
        copy.start()

    def load_more(g, carry):
        load(g).start()
        return carry

    lax.fori_loop(TAPS, FR, load_more, 0)

    halo = pltpu.make_async_remote_copy(
        src_ref=volt_hbm.at[pl.ds(FR - HISTORY, HISTORY)],
        dst_ref=volt.at[pl.ds(0, HISTORY)],
        send_sem=halo_sem.at[0],
        recv_sem=halo_sem.at[1],
        device_id={"tm": after},
        device_id_type=MESH_ID,
    )

    def spectrum(g):
        def chunk(i, carry):
            rows = pl.ds(pl.multiple_of(i * 16, 16), 16)
            total = w[0:1, :] * volt[g, rows, :].astype(jnp.float32)
            for tap in range(1, TAPS):
                total = total + w[tap : tap + 1, :] * volt[g + tap, rows, :].astype(jnp.float32)
            weighted[rows, :] = total.astype(jnp.bfloat16)
            return carry

        lax.fori_loop(0, RHERE * C // 16, chunk, 0, unroll=2)
        for pair in range(RHERE // 2):
            out = lax.dot_general(
                fine[...],
                weighted[pair * 2 * C : (pair + 1) * 2 * C, :],
                (((1,), (1,)), ((), ())),
                preferred_element_type=jnp.float32,
            ).reshape(NROW, 2, KHERE, 2 * C)
            for q in range(2):
                both = jnp.concatenate([out[:, q, :, :C], out[:, q, :, C:]], axis=1)
                send[g, :, pair * 2 * KHERE : (pair + 1) * 2 * KHERE, q * C : (q + 1) * C] = (
                    both.astype(jnp.bfloat16)
                )

    def dispatch(g):
        def one(e, carry):
            to = partner(e)
            pltpu.make_async_remote_copy(
                src_ref=send.at[g, to],
                dst_ref=recv.at[g, me],
                send_sem=send_sem.at[g],
                recv_sem=recv_sem.at[g],
                device_id={"row": to},
                device_id_type=MESH_ID,
            ).start()
            return carry

        lax.fori_loop(0, NROW - 1, one, 0)
        pltpu.make_async_copy(send.at[g, me], recv.at[g, me], recv_sem.at[g]).start()

    def beams(g):
        pltpu.make_async_copy(send.at[g], recv.at[g], recv_sem.at[g]).wait()
        for part in range(4):
            rows = R * KHERE // 4
            block = recv[g, pl.ds(part * NROW // 4, NROW // 4)].reshape(rows, 2 * C)
            out = jnp.dot(block, col[...], preferred_element_type=jnp.float32)
            for q in range(2):
                mid[q, part * rows : (part + 1) * rows, :] = out[:, q * C : (q + 1) * C]
        for pair in range(KHERE // 2):
            sides = []
            for k in (2 * pair, 2 * pair + 1):
                parts = [mid[q, pl.ds(k, R, stride=KHERE), :] for q in range(2)]
                sides.append(jnp.concatenate(parts, axis=0).astype(jnp.bfloat16))
            field = jnp.dot(
                row[...], jnp.concatenate(sides, axis=1), preferred_element_type=jnp.float32
            )
            power = field[:R] * field[:R] + field[R:] * field[R:]
            for i in range(2):
                acc[2 * pair + i] += power[:, i * C : (i + 1) * C]

    table_copies[0].wait()
    for g in range(TAPS):
        load(g).wait()
    table_copies[1].wait()
    spectrum(HISTORY)
    pl.semaphore_wait(barrier, NROW - 1 + 2)
    dispatch(HISTORY)
    halo.start()

    def ahead(g, carry):
        load(g).wait()
        spectrum(g)
        dispatch(g)
        return carry

    lax.fori_loop(TAPS, FR, ahead, 0)
    halo.wait()

    def first(g, carry):
        spectrum(g)
        dispatch(g)
        return carry

    lax.fori_loop(0, HISTORY, first, 0)

    acc[...] = jnp.zeros_like(acc)
    table_copies[2].wait()
    table_copies[3].wait()

    def gather(i, carry):
        beams((i + HISTORY) % FR)
        return carry

    lax.fori_loop(0, FR, gather, 0)
    acc[...] = acc[...] * (1.0 / FR)
    result = pltpu.make_async_copy(acc, out_hbm, out_sem.at[0])
    result.start()

    def sent(g, carry):
        some = pl.ds(0, NROW - 1)
        pltpu.make_async_copy(send.at[g, some], recv.at[g, some], send_sem.at[g]).wait()
        return carry

    lax.fori_loop(0, FR, sent, 0)
    result.wait()


def body(voltage):
    frames, rows, columns, width = voltage.shape
    any_space = pl.BlockSpec(memory_space=pl.ANY)
    fine, column, row = tables()
    power = pl.pallas_call(
        kernel,
        out_shape=jax.ShapeDtypeStruct((KHERE, R, C), jnp.float32),
        in_specs=[any_space] * 5,
        out_specs=any_space,
        scratch_shapes=[
            pltpu.VMEM((FR + HISTORY, RHERE * C, 2 * NCH), jnp.bfloat16),
            pltpu.VMEM((TAPS, 2 * NCH), jnp.float32),
            pltpu.VMEM((2 * NCH, 2 * NCH), jnp.bfloat16),
            pltpu.VMEM((2 * C, 2 * C), jnp.bfloat16),
            pltpu.VMEM((2 * R, 2 * R), jnp.bfloat16),
            pltpu.VMEM((RHERE * C, 2 * NCH), jnp.bfloat16),
            pltpu.VMEM((FR, NROW, RK, 2 * C), jnp.bfloat16),
            pltpu.VMEM((FR, NROW, RK, 2 * C), jnp.bfloat16),
            pltpu.VMEM((2, R * KHERE, C), jnp.float32),
            pltpu.VMEM((KHERE, R, C), jnp.float32),
            pltpu.SemaphoreType.DMA((FR,)),
            pltpu.SemaphoreType.DMA((4,)),
            pltpu.SemaphoreType.DMA((2,)),
            pltpu.SemaphoreType.DMA((FR,)),
            pltpu.SemaphoreType.DMA((FR,)),
            pltpu.SemaphoreType.DMA((1,)),
        ],
        compiler_params=pltpu.CompilerParams(
            collective_id=0, has_side_effects=True, vmem_limit_bytes=48 * 1024 * 1024
        ),
        name="beamformer",
    )(
        voltage.reshape(frames, rows * columns, width),
        jnp.asarray(pfb_window()),
        jnp.asarray(fine),
        jnp.asarray(column),
        jnp.asarray(row),
    )
    return power[None]


def solution(mesh):
    return jax.shard_map(
        body,
        mesh=mesh,
        in_specs=(P("tm", "row", None, None),),
        out_specs=P("tm", "row", None, None),
        check_vma=False,
    )
```

time: 315 us -> 199 us (0.63)
  waiting for transfers between devices: 216 us -> 0 us
  Pallas kernels: 0 us -> 194 us
  local copies, waits for them, and re-layouts: 51.2 us -> 4.34 us
  matrix products: 26.3 us -> 0 us
  starting transfers between devices: 15 us -> 0 us
  other arithmetic: 3.66 us -> 0 us
    pallas_call x0 -> x1, Pallas kernels: none -> 194 us  [body(): pl.pallas_call(kernel, out_shape=jax.ShapeDtypeStruct((KHERE, R, C), jnp....]
    all_to_all x1 -> x0, waiting for transfers between devices: 183 us -> none  [body(): lax.all_to_all(spectrum, 'row', split_axis=3, concat_axis=1, tiled=True)]
    ppermute x1 -> x0, waiting for transfers between devices: 33.1 us -> none  [shifted(): return lax.ppermute(value, axis, pairs)]
    dot_general x2 -> x0, matrix products: 26.3 us -> none  [the longest x1 16.7 us: body(): jnp.einsum('fdcs,sq->fdqc', weighted, fine_table, preferred_element_type=...]
    all_to_all x2 -> x0, local copies, waits for them, and re-layouts: 25.5 us -> none  [body(): lax.all_to_all(spectrum, 'row', split_axis=3, concat_axis=1, tiled=True)]
    reshape x1 -> x0, local copies, waits for them, and re-layouts: 13.1 us -> none  [body(): spectrum.astype(jnp.bfloat16)]
    all_to_all x1 -> x0, starting transfers between devices: 12.9 us -> none  [body(): lax.all_to_all(spectrum, 'row', split_axis=3, concat_axis=1, tiled=True)]
    concatenate x1 -> x0, local copies, waits for them, and re-layouts: 7.72 us -> none  [body(): extended = jnp.concatenate([earlier, voltage], axis=0)]
  transfers between devices with their start and end apart: 2 -> 0, of which waited for: 2 -> 0; matrix products, arithmetic and copies ran while one was open for 1% -> 0% of each run, Pallas kernels for 0% -> 0%
where the time goes in v1:
time: 199 us
  Pallas kernels  194 us (97%)
  local copies, waits for them, and re-layouts  4.34 us (2%)
    pallas_call x1, Pallas kernels, body(): pl.pallas_call(kernel, out_shape=jax.ShapeDtypeStruct((KHERE, R, C), jnp....  194 us
    unnamed x9, local copies, waits for them, and re-layouts  4.34 us

profile of v1, /device:TPU:1, one launch (start us, length us, event | category | flops | bytes accessed | tf_op | source)
XLA Modules:
  0.0 198.5 jit_solution(2342009303912043757)
XLA Ops:
  0.0 0.0 copy-start
  0.0 1.0 copy-done
  1.0 0.0 copy-start.1
  1.0 0.9 copy-done.1
  1.9 0.0 copy-start.2
  1.9 0.9 copy-done.2
  2.9 0.0 copy-start.3
  2.9 0.7 copy-done.3
  3.5 194.2 %beamformer.1 = f32[8,128,128]{2,1,0:T(8,128)S(1)} custom-call(bf16[16,512,512]{2,1,0:T(8,128)(2,1)} %bitcast.3, f32[4,512]{1,0:T(4,128)S(1)} %copy-done.3, bf16[512,512]{1,0:T(8,128)(2,1)S(1)} %copy-done, bf16[256,256]{1,0:T(8,128)(2,1)S(1)} %copy-done.2, bf16[256,256]{1,0:T(8,128)(2,1)S(1)} %copy-done.1), custom_call_target="tpu_custom_call" | custom-call | tf_op jit(solution)/shard_map/beamformer/pallas_call | solution.py:218
  197.7 0.8 copy.7
Async XLA Ops:
  0.0 1.0 copy-start
  1.0 0.9 copy-start.1
  1.9 0.9 copy-start.2
  2.9 0.7 copy-start.3

commit v2 on v1

v2 whole, which is shorter than its diff:
```python
import math

import jax
import jax.numpy as jnp
import ml_dtypes
import numpy as np
from jax import lax
from jax.experimental import pallas as pl
from jax.experimental.pallas import tpu as pltpu
from jax.sharding import PartitionSpec as P

TAPS = 4
HISTORY = TAPS - 1
NCH = 256
C = 128
R = 128
FR = 16
NROW = 32
NTM = 8
RHERE = R // NROW
KHERE = NCH // NROW
RK = RHERE * KHERE
VMEM_BYTES = 54656 * 1024
MESH_ID = pl.DeviceIdType.MESH


def pfb_window():
    points = np.arange(TAPS * NCH, dtype=np.float64)
    offset = (points + 0.5) / NCH - TAPS / 2.0
    taper = 0.5 - 0.5 * np.cos(2.0 * math.pi * (points + 0.5) / (TAPS * NCH))
    shaped = (np.sinc(offset) * taper).reshape(TAPS, NCH)
    return np.concatenate([shaped, shaped], axis=1).astype(np.float32)


def dft_table(length):
    indices = np.arange(length)
    angle = (indices[:, None] * indices[None, :] % length) * (2.0 * math.pi / length)
    cosine = np.cos(angle) / math.sqrt(length)
    sine = np.sin(angle) / math.sqrt(length)
    upper = np.stack([cosine, -sine], axis=1)
    bottom = np.stack([sine, cosine], axis=1)
    return np.stack([upper, bottom], axis=0).astype(np.float32).astype(ml_dtypes.bfloat16)


def tables():
    fine = dft_table(NCH).reshape(2 * NCH, 2, NROW, KHERE).transpose(2, 1, 3, 0)
    fine = fine.reshape(2 * NCH, 2 * NCH)
    column = dft_table(C).reshape(2 * C, 2 * C)
    row = dft_table(R).transpose(2, 3, 0, 1).reshape(2 * R, 2 * R)
    rest, parts = pfb_window(), []
    for _ in range(3):
        parts.append(rest.astype(ml_dtypes.bfloat16))
        rest = rest - parts[-1].astype(np.float32)
    assert not rest.any()
    parts.append(np.zeros_like(parts[0]))
    return np.concatenate([fine, np.concatenate([column, row], axis=1)] + parts, axis=0)


def kernel(
    volt_hbm, table_hbm, acc,
    volt, window, fine, beam, weighted, send, recv, mid,
    load_sem, table_sem, halo_sem, send_sem, recv_sem,
):
    tm = lax.axis_index("tm")
    me = lax.axis_index("row")
    x, z, core = me // 16, (me // 2) % 8, me % 2
    after, before = (tm + 1) % NTM, (tm + NTM - 1) % NTM

    def partner(e):
        i = e // 4
        dz = 4 + (i + 1) // 2 * (1 - i % 2 * 2)
        dx = 1 - (e // 2) % 2
        dc = 1 - e % 2
        return (((x + dx) % 2) * 8 + (z + dz) % 8) * 2 + (core + dc) % 2

    def load(g):
        return pltpu.make_async_copy(volt_hbm.at[g], volt.at[g + HISTORY], load_sem.at[g])

    def load_half(g, half):
        rows = pl.ds(half * 2 * C, 2 * C)
        return pltpu.make_async_copy(
            volt_hbm.at[g, rows], volt.at[g + HISTORY, rows], load_sem.at[g + FR * half]
        )

    window_copy, fine_copy, beam_copy = [
        pltpu.make_async_copy(table_hbm.at[pl.ds(start, ref.shape[0])], ref, table_sem.at[i])
        for i, (start, ref) in enumerate(
            ((2 * NCH + 2 * C, window), (0, fine), (2 * NCH, beam))
        )
    ]
    window_copy.start()
    for g in range(TAPS):
        load_half(g, 0).start()
    fine_copy.start()

    barrier = pltpu.get_barrier_semaphore()

    def greet(e, carry):
        pl.semaphore_signal(barrier, inc=1, device_id={"row": partner(e)}, device_id_type=MESH_ID)
        return carry

    lax.fori_loop(0, NROW - 1, greet, 0)
    for neighbour in (before, after):
        pl.semaphore_signal(barrier, inc=1, device_id={"tm": neighbour}, device_id_type=MESH_ID)

    for g in range(TAPS):
        load_half(g, 1).start()

    def load_more(g, carry):
        load(g).start()
        return carry

    lax.fori_loop(TAPS, FR, load_more, 0)
    beam_copy.start()

    halo = pltpu.make_async_remote_copy(
        src_ref=volt_hbm.at[pl.ds(FR - HISTORY, HISTORY)],
        dst_ref=volt.at[pl.ds(0, HISTORY)],
        send_sem=halo_sem.at[0],
        recv_sem=halo_sem.at[1],
        device_id={"tm": after},
        device_id_type=MESH_ID,
    )

    def spectrum(g, half):
        parts = window[...].astype(jnp.float32)
        w = parts[:TAPS] + parts[TAPS : 2 * TAPS] + parts[2 * TAPS : 3 * TAPS]

        def chunk(i, carry):
            rows = pl.ds(pl.multiple_of(half * 2 * C + i * 16, 16), 16)
            total = w[0:1] * volt[g, rows, :].astype(jnp.float32)
            for tap in range(1, TAPS):
                total = total + w[tap : tap + 1] * volt[g + tap, rows, :].astype(jnp.float32)
            weighted[rows, :] = total.astype(jnp.bfloat16)
            return carry

        lax.fori_loop(0, 2 * C // 16, chunk, 0, unroll=2)
        out = lax.dot_general(
            fine[...],
            weighted[half * 2 * C : (half + 1) * 2 * C, :],
            (((1,), (1,)), ((), ())),
            preferred_element_type=jnp.float32,
        ).reshape(NROW, 2, KHERE, 2 * C)
        for q in range(2):
            both = jnp.concatenate([out[:, q, :, :C], out[:, q, :, C:]], axis=1)
            send[g, :, half * RK // 2 : (half + 1) * RK // 2, q * C : (q + 1) * C] = (
                both.astype(jnp.bfloat16)
            )

    def dispatch(g, rows):
        def one(e, carry):
            to = partner(e)
            pltpu.make_async_remote_copy(
                src_ref=send.at[g, to, rows],
                dst_ref=recv.at[g, me, rows],
                send_sem=send_sem.at[g],
                recv_sem=recv_sem.at[g],
                device_id={"row": to},
                device_id_type=MESH_ID,
            ).start()
            return carry

        lax.fori_loop(0, NROW - 1, one, 0)
        pltpu.make_async_copy(send.at[g, me, rows], recv.at[g, me, rows], recv_sem.at[g]).start()

    def beams(g):
        pltpu.make_async_copy(send.at[g], recv.at[g], recv_sem.at[g]).wait()
        for part in range(4):
            rows = R * KHERE // 4
            block = recv[g, pl.ds(part * NROW // 4, NROW // 4)].reshape(rows, 2 * C)
            out = jnp.dot(block, beam[:, : 2 * C], preferred_element_type=jnp.float32)
            for q in range(2):
                mid[q, part * rows : (part + 1) * rows, :] = out[:, q * C : (q + 1) * C]
        for pair in range(KHERE // 2):
            sides = []
            for k in (2 * pair, 2 * pair + 1):
                parts = [mid[q, pl.ds(k, R, stride=KHERE), :] for q in range(2)]
                sides.append(jnp.concatenate(parts, axis=0).astype(jnp.bfloat16))
            field = jnp.dot(
                beam[:, 2 * C :], jnp.concatenate(sides, axis=1), preferred_element_type=jnp.float32
            )
            power = (field[:R] * field[:R] + field[R:] * field[R:]) * (1.0 / FR)
            for i in range(2):
                acc[2 * pair + i] += power[:, i * C : (i + 1) * C]

    window_copy.wait()
    for half in range(2):
        for g in range(TAPS):
            load_half(g, half).wait()
        if half == 0:
            fine_copy.wait()
        spectrum(HISTORY, half)
        if half == 0:
            pl.semaphore_wait(barrier, NROW - 1 + 2)
        dispatch(HISTORY, pl.ds(half * RK // 2, RK // 2))
    halo.start()

    def forward(g):
        for half in range(2):
            spectrum(g, half)
        dispatch(g, pl.ds(0, RK))

    def ahead(g, carry):
        load(g).wait()
        forward(g)
        return carry

    lax.fori_loop(TAPS, FR, ahead, 0)
    halo.wait()

    def first(g, carry):
        forward(g)
        return carry

    lax.fori_loop(0, HISTORY, first, 0)

    acc[...] = jnp.zeros_like(acc)
    beam_copy.wait()

    def gather(i, carry):
        beams((i + HISTORY) % FR)
        return carry

    lax.fori_loop(0, FR, gather, 0)

    def sent(g, carry):
        some = pl.ds(0, NROW - 1)
        pltpu.make_async_copy(send.at[g, some], recv.at[g, some], send_sem.at[g]).wait()
        return carry

    lax.fori_loop(0, FR, sent, 0)


def body(voltage):
    frames, rows, columns, width = voltage.shape
    in_hbm = pl.BlockSpec(memory_space=pltpu.HBM)
    power = pl.pallas_call(
        kernel,
        out_shape=jax.ShapeDtypeStruct((KHERE, R, C), jnp.float32),
        in_specs=[in_hbm] * 2,
        out_specs=pl.BlockSpec(memory_space=pltpu.VMEM),
        scratch_shapes=[
            pltpu.VMEM((FR + HISTORY, RHERE * C, 2 * NCH), jnp.bfloat16),
            pltpu.VMEM((4 * TAPS, 2 * NCH), jnp.bfloat16),
            pltpu.VMEM((2 * NCH, 2 * NCH), jnp.bfloat16),
            pltpu.VMEM((2 * C, 4 * C), jnp.bfloat16),
            pltpu.VMEM((RHERE * C, 2 * NCH), jnp.bfloat16),
            pltpu.VMEM((FR, NROW, RK, 2 * C), jnp.bfloat16),
            pltpu.VMEM((FR, NROW, RK, 2 * C), jnp.bfloat16),
            pltpu.VMEM((2, R * KHERE, C), jnp.float32),
            pltpu.SemaphoreType.DMA((FR + HISTORY + 1,)),
            pltpu.SemaphoreType.DMA((3,)),
            pltpu.SemaphoreType.DMA((2,)),
            pltpu.SemaphoreType.DMA((FR,)),
            pltpu.SemaphoreType.DMA((FR,)),
        ],
        compiler_params=pltpu.CompilerParams(
            collective_id=0, has_side_effects=True, vmem_limit_bytes=VMEM_BYTES
        ),
        name="beamformer",
    )(
        voltage.reshape(frames, rows * columns, width),
        jnp.asarray(tables()),
    )
    return power[None]


def solution(mesh):
    return jax.shard_map(
        body,
        mesh=mesh,
        in_specs=(P("tm", "row", None, None),),
        out_specs=P("tm", "row", None, None),
        check_vma=False,
    )
```

time: 199 us -> 196 us (0.985)
  local copies, waits for them, and re-layouts: 4.34 us -> 0.8 us
    unnamed x9 -> x1, local copies, waits for them, and re-layouts: 4.34 us -> 0.8 us
where the time goes in v2:
time: 196 us
  Pallas kernels  195 us (99%)
    pallas_call x1, Pallas kernels, body(): pl.pallas_call(kernel, out_shape=jax.ShapeDtypeStruct((KHERE, R, C), jnp....  195 us

profile of v2, /device:TPU:1, one launch (start us, length us, event | category | flops | bytes accessed | tf_op | source)
XLA Modules:
  0.0 195.6 jit_solution(8308722119480197603)
XLA Ops:
  0.0 194.8 %beamformer.1 = f32[8,128,128]{2,1,0:T(8,128)S(1)} custom-call(bf16[16,512,512]{2,1,0:T(8,128)(2,1)} %bitcast.3, bf16[784,512]{1,0:T(8,128)(2,1)} %constant.2.clone.table_hbm), custom_call_target="tpu_custom_call" | custom-call | tf_op jit(solution)/shard_map/beamformer/pallas_call | solution.py:237
  194.8 0.8 copy.4

commit v3 on v2

--- a/solution.py
+++ b/solution.py
@@ -59,7 +59,7 @@
 def kernel(
     volt_hbm, table_hbm, acc,
     volt, window, fine, beam, weighted, send, recv, mid,
-    load_sem, table_sem, halo_sem, send_sem, recv_sem,
+    load_sem, table_sem, halo_sem, send_sem, recv_sem, go_sem,
 ):
     tm = lax.axis_index("tm")
     me = lax.axis_index("row")
@@ -95,13 +95,18 @@
 
     barrier = pltpu.get_barrier_semaphore()
 
+    def signal(sem, **device_id):
+        pl.semaphore_signal(sem, inc=1, device_id=device_id, device_id_type=MESH_ID)
+
     def greet(e, carry):
-        pl.semaphore_signal(barrier, inc=1, device_id={"row": partner(e)}, device_id_type=MESH_ID)
-        return carry
-
-    lax.fori_loop(0, NROW - 1, greet, 0)
-    for neighbour in (before, after):
-        pl.semaphore_signal(barrier, inc=1, device_id={"tm": neighbour}, device_id_type=MESH_ID)
+        signal(barrier, row=partner(2 * e + 1) // 2 * 2)
+        return carry
+
+    lax.fori_loop(0, NROW // 2 - 1, greet, 0)
+
+    @pl.when(core == 1)
+    def _():
+        signal(barrier, row=me - 1)
 
     for g in range(TAPS):
         load_half(g, 1).start()
@@ -183,6 +188,27 @@
             for i in range(2):
                 acc[2 * pair + i] += power[:, i * C : (i + 1) * C]
 
+    def enter():
+        @pl.when(core == 0)
+        def _():
+            pl.semaphore_wait(barrier, NROW - 1)
+            signal(go_sem.at[0], row=me + 1)
+
+        @pl.when(core == 1)
+        def _():
+            pl.semaphore_wait(go_sem.at[0], 1)
+            signal(barrier, tm=before)
+
+    def meet_next_slab():
+        @pl.when(core == 1)
+        def _():
+            pl.semaphore_wait(barrier, 1)
+            signal(go_sem.at[1], row=me - 1)
+
+        @pl.when(core == 0)
+        def _():
+            pl.semaphore_wait(go_sem.at[1], 1)
+
     window_copy.wait()
     for half in range(2):
         for g in range(TAPS):
@@ -191,9 +217,8 @@
             fine_copy.wait()
         spectrum(HISTORY, half)
         if half == 0:
-            pl.semaphore_wait(barrier, NROW - 1 + 2)
+            enter()
         dispatch(HISTORY, pl.ds(half * RK // 2, RK // 2))
-    halo.start()
 
     def forward(g):
         for half in range(2):
@@ -205,7 +230,10 @@
         forward(g)
         return carry
 
-    lax.fori_loop(TAPS, FR, ahead, 0)
+    lax.fori_loop(TAPS, TAPS + 2, ahead, 0)
+    meet_next_slab()
+    halo.start()
+    lax.fori_loop(TAPS + 2, FR, ahead, 0)
     halo.wait()
 
     def first(g, carry):
@@ -253,6 +281,7 @@
             pltpu.SemaphoreType.DMA((2,)),
             pltpu.SemaphoreType.DMA((FR,)),
             pltpu.SemaphoreType.DMA((FR,)),
+            pltpu.SemaphoreType.REGULAR((2,)),
         ],
         compiler_params=pltpu.CompilerParams(
             collective_id=0, has_side_effects=True, vmem_limit_bytes=VMEM_BYTES

time: 196 us -> 194 us (0.990)
  Pallas kernels: 195 us -> 193 us
    pallas_call x1, Pallas kernels: 195 us -> 193 us  [body(): pl.pallas_call(kernel, out_shape=jax.ShapeDtypeStruct((KHERE, R, C), jnp....]
where the time goes in v3:
time: 194 us; the launch traced here: 193 us
  Pallas kernels  193 us (99%)
    pallas_call x1, Pallas kernels, body(): pl.pallas_call(kernel, out_shape=jax.ShapeDtypeStruct((KHERE, R, C), jnp....  193 us

profile of v3, /device:TPU:1, one launch (start us, length us, event | category | flops | bytes accessed | tf_op | source)
XLA Modules:
  0.0 193.5 jit_solution(6428071063447792911)
XLA Ops:
  0.0 192.7 %beamformer.1 = f32[8,128,128]{2,1,0:T(8,128)S(1)} custom-call(bf16[16,512,512]{2,1,0:T(8,128)(2,1)} %bitcast.3, bf16[784,512]{1,0:T(8,128)(2,1)} %constant.2.clone.table_hbm), custom_call_target="tpu_custom_call" | custom-call | tf_op jit(solution)/shard_map/beamformer/pallas_call | solution.py:265
  192.7 0.8 copy.4

commit v4 on v3

--- a/solution.py
+++ b/solution.py
@@ -20,6 +20,9 @@
 RHERE = R // NROW
 KHERE = NCH // NROW
 RK = RHERE * KHERE
+PARTS = 4
+PART = NROW // PARTS
+FAR = 5
 VMEM_BYTES = 54656 * 1024
 MESH_ID = pl.DeviceIdType.MESH
 
@@ -66,12 +69,15 @@
     x, z, core = me // 16, (me // 2) % 8, me % 2
     after, before = (tm + 1) % NTM, (tm + NTM - 1) % NTM
 
-    def partner(e):
-        i = e // 4
-        dz = 4 + (i + 1) // 2 * (1 - i % 2 * 2)
-        dx = 1 - (e // 2) % 2
-        dc = 1 - e % 2
-        return (((x + dx) % 2) * 8 + (z + dz) % 8) * 2 + (core + dc) % 2
+    def plane(i):
+        return (z + 4 + (i + 1) // 2 * (1 - i % 2 * 2)) % 8
+
+    half_ring = NROW // 2
+
+    def device(there, dx, dc):
+        return (x if dx == 0 else 1 - x) * half_ring + 2 * there + (core if dc == 0 else 1 - core)
+
+    SPOTS = ((1, 1), (1, 0), (0, 1), (0, 0))
 
     def load(g):
         return pltpu.make_async_copy(volt_hbm.at[g], volt.at[g + HISTORY], load_sem.at[g])
@@ -82,31 +88,55 @@
             volt_hbm.at[g, rows], volt.at[g + HISTORY, rows], load_sem.at[g + FR * half]
         )
 
-    window_copy, fine_copy, beam_copy = [
+    window_copy, *fine_copies, beam_copy = [
         pltpu.make_async_copy(table_hbm.at[pl.ds(start, ref.shape[0])], ref, table_sem.at[i])
         for i, (start, ref) in enumerate(
-            ((2 * NCH + 2 * C, window), (0, fine), (2 * NCH, beam))
+            (
+                (2 * NCH + 2 * C, window),
+                (0, fine.at[pl.ds(0, NCH)]),
+                (NCH, fine.at[pl.ds(NCH, NCH)]),
+                (2 * NCH, beam),
+            )
         )
     ]
     window_copy.start()
     for g in range(TAPS):
         load_half(g, 0).start()
-    fine_copy.start()
+    for copy in fine_copies:
+        copy.start()
 
     barrier = pltpu.get_barrier_semaphore()
+    near_ear, slab_ear = 2 * z + 1, NROW // 2 + 2 * z + 1
+    is_near_ear, is_slab_ear = me == near_ear, me == slab_ear
 
     def signal(sem, **device_id):
         pl.semaphore_signal(sem, inc=1, device_id=device_id, device_id_type=MESH_ID)
 
-    def greet(e, carry):
-        signal(barrier, row=partner(2 * e + 1) // 2 * 2)
+    def tell_plane(sem, ear):
+        chip = ear - 1
+        signal(sem, row=chip)
+        signal(sem, row=(chip + NROW // 2) % NROW)
+        signal(sem, row=(ear + NROW // 2) % NROW)
+
+    def greet(i, carry):
+        there = plane(i)
+        for side in range(2):
+            signal(barrier, row=side * half_ring + 2 * there)
         return carry
 
-    lax.fori_loop(0, NROW // 2 - 1, greet, 0)
+    for dz in (1, 7):
+        signal(barrier, row=2 * ((z + dz) % 8) + 1)
+
+    @pl.when(jnp.logical_not(is_near_ear))
+    def _():
+        signal(barrier, row=near_ear)
 
     @pl.when(core == 1)
     def _():
         signal(barrier, row=me - 1)
+
+    signal(barrier, row=(1 - x) * half_ring + 2 * z)
+    lax.fori_loop(0, 7, greet, 0)
 
     for g in range(TAPS):
         load_half(g, 1).start()
@@ -127,6 +157,11 @@
         device_id_type=MESH_ID,
     )
 
+    everything = pl.ds(0, RK)
+
+    def half_of_block(half):
+        return pl.ds(pl.multiple_of(half * (RK // 2), RK // 2), RK // 2)
+
     def spectrum(g, half):
         parts = window[...].astype(jnp.float32)
         w = parts[:TAPS] + parts[TAPS : 2 * TAPS] + parts[2 * TAPS : 3 * TAPS]
@@ -136,25 +171,22 @@
             total = w[0:1] * volt[g, rows, :].astype(jnp.float32)
             for tap in range(1, TAPS):
                 total = total + w[tap : tap + 1] * volt[g + tap, rows, :].astype(jnp.float32)
-            weighted[rows, :] = total.astype(jnp.bfloat16)
+            weighted[pl.ds(pl.multiple_of(i * 16, 16), 16), :] = total.astype(jnp.bfloat16)
             return carry
 
         lax.fori_loop(0, 2 * C // 16, chunk, 0, unroll=2)
         out = lax.dot_general(
             fine[...],
-            weighted[half * 2 * C : (half + 1) * 2 * C, :],
+            weighted[...],
             (((1,), (1,)), ((), ())),
             preferred_element_type=jnp.float32,
         ).reshape(NROW, 2, KHERE, 2 * C)
         for q in range(2):
             both = jnp.concatenate([out[:, q, :, :C], out[:, q, :, C:]], axis=1)
-            send[g, :, half * RK // 2 : (half + 1) * RK // 2, q * C : (q + 1) * C] = (
-                both.astype(jnp.bfloat16)
-            )
-
-    def dispatch(g, rows):
-        def one(e, carry):
-            to = partner(e)
+            send[g, :, half_of_block(half), q * C : (q + 1) * C] = both.astype(jnp.bfloat16)
+
+    def dispatch(g, rows, start, end):
+        def post(to):
             pltpu.make_async_remote_copy(
                 src_ref=send.at[g, to, rows],
                 dst_ref=recv.at[g, me, rows],
@@ -163,16 +195,29 @@
                 device_id={"row": to},
                 device_id_type=MESH_ID,
             ).start()
+
+        def one(i, carry):
+            there = plane(i)
+            for dx, dc in SPOTS:
+                post(device(there, dx, dc))
             return carry
 
-        lax.fori_loop(0, NROW - 1, one, 0)
-        pltpu.make_async_copy(send.at[g, me, rows], recv.at[g, me, rows], recv_sem.at[g]).start()
+        lax.fori_loop(start, min(end, 7), one, 0)
+        if end == 8:
+            for dx, dc in SPOTS[:3]:
+                post(device(z, dx, dc))
+
+    def keep(g):
+        pltpu.make_async_copy(
+            send.at[g, me], recv.at[g, me], recv_sem.at[g]
+        ).start()
 
     def beams(g):
         pltpu.make_async_copy(send.at[g], recv.at[g], recv_sem.at[g]).wait()
-        for part in range(4):
-            rows = R * KHERE // 4
-            block = recv[g, pl.ds(part * NROW // 4, NROW // 4)].reshape(rows, 2 * C)
+        for part in range(PARTS):
+            rows = R * KHERE // PARTS
+            sources = pl.ds(part * PART, PART)
+            block = recv[g, sources].reshape(rows, 2 * C)
             out = jnp.dot(block, beam[:, : 2 * C], preferred_element_type=jnp.float32)
             for q in range(2):
                 mid[q, part * rows : (part + 1) * rows, :] = out[:, q * C : (q + 1) * C]
@@ -188,75 +233,117 @@
             for i in range(2):
                 acc[2 * pair + i] += power[:, i * C : (i + 1) * C]
 
+    def enter_near():
+        @pl.when(is_near_ear)
+        def _():
+            pl.semaphore_wait(barrier, 3 + 2 * 4)
+            tell_plane(go_sem.at[0], near_ear)
+
+        @pl.when(jnp.logical_not(is_near_ear))
+        def _():
+            pl.semaphore_wait(go_sem.at[0], 1)
+
     def enter():
         @pl.when(core == 0)
         def _():
             pl.semaphore_wait(barrier, NROW - 1)
-            signal(go_sem.at[0], row=me + 1)
+            signal(go_sem.at[1], row=me + 1)
 
         @pl.when(core == 1)
         def _():
-            pl.semaphore_wait(go_sem.at[0], 1)
+            pl.semaphore_wait(go_sem.at[1], 1)
+
+        @pl.when(is_slab_ear)
+        def _():
             signal(barrier, tm=before)
 
     def meet_next_slab():
-        @pl.when(core == 1)
+        @pl.when(is_slab_ear)
         def _():
             pl.semaphore_wait(barrier, 1)
-            signal(go_sem.at[1], row=me - 1)
-
-        @pl.when(core == 0)
-        def _():
-            pl.semaphore_wait(go_sem.at[1], 1)
-
-    window_copy.wait()
-    for half in range(2):
-        for g in range(TAPS):
-            load_half(g, half).wait()
-        if half == 0:
-            fine_copy.wait()
-        spectrum(HISTORY, half)
-        if half == 0:
+            tell_plane(go_sem.at[2], slab_ear)
+
+        @pl.when(jnp.logical_not(is_slab_ear))
+        def _():
+            pl.semaphore_wait(go_sem.at[2], 1)
+
+    acc[...] = jnp.zeros_like(acc)
+
+    def produce(n, carry):
+        g, half = (n // 2 + HISTORY) % FR, n % 2
+
+        @pl.when(n == 0)
+        def _():
+            window_copy.wait()
+            for i in range(TAPS):
+                load_half(i, 0).wait()
+            for copy in fine_copies:
+                copy.wait()
+
+        @pl.when(n == 1)
+        def _():
+            for i in range(TAPS):
+                load_half(i, 1).wait()
+
+        @pl.when((n > 1) & (half == 0) & (g >= TAPS))
+        def _():
+            load(g).wait()
+
+        @pl.when(n == 2 * (FR - HISTORY))
+        def _():
+            halo.wait()
+
+        spectrum(g, half)
+
+        @pl.when(n == 0)
+        def _():
+            enter_near()
+
+        @pl.when(n < 4)
+        def _():
+            dispatch(g, half_of_block(half), FAR, 8)
+
+        @pl.when(n == 3)
+        def _():
             enter()
-        dispatch(HISTORY, pl.ds(half * RK // 2, RK // 2))
-
-    def forward(g):
-        for half in range(2):
-            spectrum(g, half)
-        dispatch(g, pl.ds(0, RK))
-
-    def ahead(g, carry):
-        load(g).wait()
-        forward(g)
+
+            def rest(f, carry):
+                dispatch(f, everything, 0, FAR)
+                keep(f)
+                return carry
+
+            lax.fori_loop(HISTORY, HISTORY + 2, rest, 0)
+
+        @pl.when((n > 3) & (half == 1))
+        def _():
+            dispatch(g, everything, 0, 8)
+            keep(g)
+
+        @pl.when(n == 7)
+        def _():
+            meet_next_slab()
+            halo.start()
+
         return carry
 
-    lax.fori_loop(TAPS, TAPS + 2, ahead, 0)
-    meet_next_slab()
-    halo.start()
-    lax.fori_loop(TAPS + 2, FR, ahead, 0)
-    halo.wait()
-
-    def first(g, carry):
-        forward(g)
-        return carry
-
-    lax.fori_loop(0, HISTORY, first, 0)
-
-    acc[...] = jnp.zeros_like(acc)
+    lax.fori_loop(0, 2 * FR, produce, 0)
     beam_copy.wait()
+
+    def sent(g):
+        some = pl.ds(0, NROW - 1)
+        pltpu.make_async_copy(send.at[g, some], recv.at[g, some], send_sem.at[g]).wait()
 
     def gather(i, carry):
         beams((i + HISTORY) % FR)
+
+        @pl.when(i < FR - 1)
+        def _():
+            sent((i + HISTORY) % FR)
+
         return carry
 
     lax.fori_loop(0, FR, gather, 0)
-
-    def sent(g, carry):
-        some = pl.ds(0, NROW - 1)
-        pltpu.make_async_copy(send.at[g, some], recv.at[g, some], send_sem.at[g]).wait()
-        return carry
-
-    lax.fori_loop(0, FR, sent, 0)
+    sent(HISTORY - 1)
 
 
 def body(voltage):
@@ -272,16 +359,16 @@
             pltpu.VMEM((4 * TAPS, 2 * NCH), jnp.bfloat16),
             pltpu.VMEM((2 * NCH, 2 * NCH), jnp.bfloat16),
             pltpu.VMEM((2 * C, 4 * C), jnp.bfloat16),
-            pltpu.VMEM((RHERE * C, 2 * NCH), jnp.bfloat16),
+            pltpu.VMEM((RHERE * C // 2, 2 * NCH), jnp.bfloat16),
             pltpu.VMEM((FR, NROW, RK, 2 * C), jnp.bfloat16),
             pltpu.VMEM((FR, NROW, RK, 2 * C), jnp.bfloat16),
             pltpu.VMEM((2, R * KHERE, C), jnp.float32),
             pltpu.SemaphoreType.DMA((FR + HISTORY + 1,)),
-            pltpu.SemaphoreType.DMA((3,)),
+            pltpu.SemaphoreType.DMA((4,)),
             pltpu.SemaphoreType.DMA((2,)),
             pltpu.SemaphoreType.DMA((FR,)),
             pltpu.SemaphoreType.DMA((FR,)),
-            pltpu.SemaphoreType.REGULAR((2,)),
+            pltpu.SemaphoreType.REGULAR((3,)),
         ],
         compiler_params=pltpu.CompilerParams(
             collective_id=0, has_side_effects=True, vmem_limit_bytes=VMEM_BYTES

time: 194 us -> 192 us (0.990)
  Pallas kernels: 193 us -> 191 us
where the time goes in v4:
time: 192 us
  Pallas kernels  191 us (99%)
    pallas_call x1, Pallas kernels, body(): pl.pallas_call(kernel, out_shape=jax.ShapeDtypeStruct((KHERE, R, C), jnp....  191 us

profile of v4, /device:TPU:1, one launch (start us, length us, event | category | flops | bytes accessed | tf_op | source)
XLA Modules:
  0.0 192.1 jit_solution(10623037939561418280)
XLA Ops:
  0.0 191.3 %beamformer.1 = f32[8,128,128]{2,1,0:T(8,128)S(1)} custom-call(bf16[16,512,512]{2,1,0:T(8,128)(2,1)} %bitcast.3, bf16[784,512]{1,0:T(8,128)(2,1)} %constant.2.clone.table_hbm), custom_call_target="tpu_custom_call" | custom-call | tf_op jit(solution)/shard_map/beamformer/pallas_call | solution.py:352
  191.3 0.8 copy.4

commit v5 on v4

--- a/solution.py
+++ b/solution.py
@@ -162,7 +162,7 @@
     def half_of_block(half):
         return pl.ds(pl.multiple_of(half * (RK // 2), RK // 2), RK // 2)
 
-    def spectrum(g, half):
+    def spectrum(g, half, before_transform):
         parts = window[...].astype(jnp.float32)
         w = parts[:TAPS] + parts[TAPS : 2 * TAPS] + parts[2 * TAPS : 3 * TAPS]
 
@@ -175,6 +175,7 @@
             return carry
 
         lax.fori_loop(0, 2 * C // 16, chunk, 0, unroll=2)
+        before_transform()
         out = lax.dot_general(
             fine[...],
             weighted[...],
@@ -233,12 +234,13 @@
             for i in range(2):
                 acc[2 * pair + i] += power[:, i * C : (i + 1) * C]
 
-    def enter_near():
+    def relay_near():
         @pl.when(is_near_ear)
         def _():
             pl.semaphore_wait(barrier, 3 + 2 * 4)
             tell_plane(go_sem.at[0], near_ear)
 
+    def enter_near():
         @pl.when(jnp.logical_not(is_near_ear))
         def _():
             pl.semaphore_wait(go_sem.at[0], 1)
@@ -277,8 +279,7 @@
             window_copy.wait()
             for i in range(TAPS):
                 load_half(i, 0).wait()
-            for copy in fine_copies:
-                copy.wait()
+            relay_near()
 
         @pl.when(n == 1)
         def _():
@@ -293,7 +294,13 @@
         def _():
             halo.wait()
 
-        spectrum(g, half)
+        def fine_ready():
+            @pl.when(n == 0)
+            def _():
+                for copy in fine_copies:
+                    copy.wait()
+
+        spectrum(g, half, fine_ready)
 
         @pl.when(n == 0)
         def _():

time: 192 us -> 193 us (level)
  no operation moved by 1% of the time
where the time goes in v5:
time: 193 us; the launch traced here: 192 us
  Pallas kernels  192 us (99%)
    pallas_call x1, Pallas kernels, body(): pl.pallas_call(kernel, out_shape=jax.ShapeDtypeStruct((KHERE, R, C), jnp....  192 us

profile of v5, /device:TPU:1, one launch (start us, length us, event | category | flops | bytes accessed | tf_op | source)
XLA Modules:
  0.0 192.5 jit_solution(14707142731638607612)
XLA Ops:
  0.0 191.7 %beamformer.1 = f32[8,128,128]{2,1,0:T(8,128)S(1)} custom-call(bf16[16,512,512]{2,1,0:T(8,128)(2,1)} %bitcast.3, bf16[784,512]{1,0:T(8,128)(2,1)} %constant.2.clone.table_hbm), custom_call_target="tpu_custom_call" | custom-call | tf_op jit(solution)/shard_map/beamformer/pallas_call | solution.py:359
  191.7 0.8 copy.4

commit v6 on v5

--- a/solution.py
+++ b/solution.py
@@ -106,8 +106,10 @@
         copy.start()
 
     barrier = pltpu.get_barrier_semaphore()
-    near_ear, slab_ear = 2 * z + 1, NROW // 2 + 2 * z + 1
+    near_ear, slab_ear = 2 * z + 1, NROW // 2 + 1
     is_near_ear, is_slab_ear = me == near_ear, me == slab_ear
+    hears_all = jnp.logical_not(is_near_ear | is_slab_ear)
+    mate_hears_all = (x == 1) & (z != 0)
 
     def signal(sem, **device_id):
         pl.semaphore_signal(sem, inc=1, device_id=device_id, device_id_type=MESH_ID)
@@ -122,6 +124,11 @@
         there = plane(i)
         for side in range(2):
             signal(barrier, row=side * half_ring + 2 * there)
+
+        @pl.when(there != 0)
+        def _():
+            signal(barrier, row=half_ring + 2 * there + 1)
+
         return carry
 
     for dz in (1, 7):
@@ -134,6 +141,10 @@
     @pl.when(core == 1)
     def _():
         signal(barrier, row=me - 1)
+
+    @pl.when((z != 0) & (me != half_ring + 2 * z + 1))
+    def _():
+        signal(barrier, row=half_ring + 2 * z + 1)
 
     signal(barrier, row=(1 - x) * half_ring + 2 * z)
     lax.fori_loop(0, 7, greet, 0)
@@ -246,12 +257,15 @@
             pl.semaphore_wait(go_sem.at[0], 1)
 
     def enter():
-        @pl.when(core == 0)
+        @pl.when(hears_all)
         def _():
             pl.semaphore_wait(barrier, NROW - 1)
+
+        @pl.when((core == 0) & jnp.logical_not(mate_hears_all))
+        def _():
             signal(go_sem.at[1], row=me + 1)
 
-        @pl.when(core == 1)
+        @pl.when(jnp.logical_not(hears_all))
         def _():
             pl.semaphore_wait(go_sem.at[1], 1)
 
@@ -263,7 +277,15 @@
         @pl.when(is_slab_ear)
         def _():
             pl.semaphore_wait(barrier, 1)
-            tell_plane(go_sem.at[2], slab_ear)
+
+            def tell(i, carry):
+                for dx, dc in SPOTS:
+                    signal(go_sem.at[2], row=device(plane(i), dx, dc))
+                return carry
+
+            lax.fori_loop(0, 7, tell, 0)
+            for dx, dc in SPOTS[:3]:
+                signal(go_sem.at[2], row=device(z, dx, dc))
 
         @pl.when(jnp.logical_not(is_slab_ear))
         def _():

time: 193 us -> 193 us (level)
  no operation moved by 1% of the time
where the time goes in v6:
time: 193 us
  Pallas kernels  192 us (99%)
    pallas_call x1, Pallas kernels, body(): pl.pallas_call(kernel, out_shape=jax.ShapeDtypeStruct((KHERE, R, C), jnp....  192 us

profile of v6, /device:TPU:1, one launch (start us, length us, event | category | flops | bytes accessed | tf_op | source)
XLA Modules:
  0.0 192.5 jit_solution(14802103957881079835)
XLA Ops:
  0.0 191.7 %beamformer.1 = f32[8,128,128]{2,1,0:T(8,128)S(1)} custom-call(bf16[16,512,512]{2,1,0:T(8,128)(2,1)} %bitcast.3, bf16[784,512]{1,0:T(8,128)(2,1)} %constant.2.clone.table_hbm), custom_call_target="tpu_custom_call" | custom-call | tf_op jit(solution)/shard_map/beamformer/pallas_call | solution.py:381
  191.7 0.8 copy.4
